TPU v7x, 32 devices: a whole 2x2x4 slice. The times are simulated.
32 devices in a mesh: grp: 4 (over x, core), dev: 8 (over z, y).
Axes of the slice: x: 2, y: 2, z: 4, core: 2. Of those that a mesh axis runs over, the one named last changes fastest.
Arguments:
- ctx_hidden: bfloat16 [512, 3584], P('dev'), may hold values from -410 to 410
- step_hidden: bfloat16 [96, 64, 3584], P(('grp', 'dev')), may hold values from -410 to 410
- norm_gain: float32 [3584], replicated, may hold values from 0.1 to 1.9
- w_query: bfloat16 [3584, 1792], P('dev'), may hold values from -4 to 4
- w_keyval: bfloat16 [3584, 512], P('dev'), may hold values from -24 to 24
- step_lengths: int32 [96], P(('grp', 'dev')), may hold values from 1 to 64, as said below
- step_mask: int32 [96, 64, 64], P(('grp', 'dev')), may hold values 0 or 1
Outputs:
- attn_out: bfloat16 [96, 64, 1792], P(('grp', 'dev'))
Inputs may be any that keep to these rules, and one draw needn't show every extreme that they name: `step_lengths`: each step's live tokens stand at its front; some solution fills all 64 slots.
All inputs are finite; a program needn't handle non-finite values. No bound on the sum of `step_mask` on one device may be relied on, other than what follows from the above.
Results may differ from a plain program's by a relative error of at most 0.009.
The roundings to bfloat16 on the way count: a program that leaves them out, or rounds other values in their place, can miss the bound.
Values may be sent and summed in bfloat16 or wider, within the bound.
A program may use at most 128 MiB of HBM per device.

v0:
```python
import math

import jax
import jax.numpy as jnp
from jax import lax
from jax.sharding import PartitionSpec as P

HEAD_SIZE = 128


NEG_FILL = -1e30


def rms_norm(hidden_rows, norm_gain):
    widened = hidden_rows.astype(jnp.float32)
    inverse = lax.rsqrt(jnp.mean(widened * widened, axis=-1, keepdims=True) + 1e-06)
    return (widened * inverse * norm_gain).astype(jnp.bfloat16)


def projector(source, incoming):
    return jnp.dot(source, incoming, preferred_element_type=jnp.float32)


def local(ctx_hidden, step_hidden, norm_gain, w_query, w_keyval, step_lengths, step_mask):
    samples, step_count, features = step_hidden.shape
    row_count = samples * step_count
    kv_cols = w_keyval.shape[1]
    key_cols = kv_cols // 2
    kv_heads = key_cols // HEAD_SIZE
    query_cols = w_query.shape[1]
    head_groups = query_cols // HEAD_SIZE // kv_heads
    score_scale = 1.0 / math.sqrt(HEAD_SIZE)
    share_rows = ctx_hidden.shape[0] // lax.axis_size("grp")
    own_context = lax.dynamic_slice_in_dim(
        ctx_hidden, lax.axis_index("grp") * share_rows, share_rows, 0
    )
    own_count = own_context.shape[0]
    normed_context = rms_norm(own_context, norm_gain)
    normed_step = rms_norm(step_hidden.reshape(row_count, features), norm_gain)
    both_rows = jnp.concatenate([normed_context, normed_step], 0)
    keyval = projector(both_rows, lax.all_gather(w_keyval, "dev", axis=0, tiled=True))
    keyval = keyval.astype(jnp.bfloat16)
    problem_keyval = keyval[:own_count]
    solution_keyval = keyval[own_count:]
    query_block = projector(normed_step, lax.all_gather(w_query, "dev", axis=0, tiled=True))
    query_block = query_block.astype(jnp.bfloat16)
    query_rows = query_block.reshape(row_count, kv_heads, head_groups, HEAD_SIZE)
    context_keys = problem_keyval[:, :key_cols]
    context_values = problem_keyval[:, key_cols:]
    context_keys, context_values = (
        lax.all_gather(context_keys, "grp", axis=0, tiled=True),
        lax.all_gather(context_values, "grp", axis=0, tiled=True),
    )
    row_top = jnp.full((row_count, kv_heads, head_groups), NEG_FILL, jnp.float32)
    key_rows = lax.all_gather(context_keys, "dev", axis=0, tiled=True).reshape(
        -1, kv_heads, HEAD_SIZE
    )
    value_rows = lax.all_gather(context_values, "dev", axis=0, tiled=True).reshape(
        -1, kv_heads, HEAD_SIZE
    )
    scores = (
        jnp.einsum("rhgd,nhd->rhgn", query_rows, key_rows, preferred_element_type=jnp.float32)
        * score_scale
    )
    new_top = jnp.maximum(row_top, scores.max(-1))
    weights = jnp.exp(scores - new_top[..., None])
    weight_sum = weights.sum(-1)
    accumulated = jnp.einsum(
        "rhgn,nhd->rhgd",
        weights.astype(jnp.bfloat16),
        value_rows,
        preferred_element_type=jnp.float32,
    )
    running = (new_top, weight_sum, accumulated)
    row_top, weight_sum, accumulated = running
    row_top = row_top.reshape(samples, step_count, kv_heads, head_groups)
    weight_sum = weight_sum.reshape(samples, step_count, kv_heads, head_groups)
    accumulated = accumulated.reshape(samples, step_count, kv_heads, head_groups, HEAD_SIZE)
    step_keys = solution_keyval[:, :key_cols].reshape(samples, step_count, kv_heads, HEAD_SIZE)
    step_values = solution_keyval[:, key_cols:].reshape(samples, step_count, kv_heads, HEAD_SIZE)
    step_queries = query_block.reshape(samples, step_count, kv_heads, head_groups, HEAD_SIZE)
    scores = (
        jnp.einsum("sthgd,suhd->sthgu", step_queries, step_keys, preferred_element_type=jnp.float32)
        * score_scale
    )
    positions = lax.iota(jnp.int32, step_count)
    causal = positions[None, :] <= positions[:, None]
    diagonal = positions[None, :] == positions[:, None]
    allowed = (
        causal[None]
        & (diagonal[None] | (step_mask == 1))
        & (positions[None, None, :] < step_lengths[:, None, None])
    )
    scores = jnp.where(allowed[:, :, None, None, :], scores, NEG_FILL)
    new_top = jnp.maximum(row_top, scores.max(-1))
    shrink = jnp.exp(row_top - new_top)
    weights = jnp.exp(scores - new_top[..., None])
    weight_sum = weight_sum * shrink + weights.sum(-1)
    accumulated = accumulated * shrink[..., None] + jnp.einsum(
        "sthgu,suhd->sthgd",
        weights.astype(jnp.bfloat16),
        step_values,
        preferred_element_type=jnp.float32,
    )
    attended = accumulated / weight_sum[..., None]
    live_rows = positions[None, :] < step_lengths[:, None]
    attended = jnp.where(live_rows[:, :, None, None, None], attended, 0.0)
    return attended.reshape(samples, step_count, query_cols).astype(jnp.bfloat16)


def solution(mesh):
    placed = (
        P("dev", None),
        P(("grp", "dev"), None, None),
        P(),
        P("dev", None),
        P("dev", None),
        P(("grp", "dev")),
        P(("grp", "dev"), None, None),
    )
    return jax.shard_map(
        local, mesh=mesh, in_specs=placed, out_specs=P(("grp", "dev"), None, None), check_vma=False
    )
```

profile of v0, /device:TPU:0, one launch (start us, length us, event | category | flops | bytes accessed | tf_op | source)
XLA Modules:
  0.0 292.5 jit_solution(13882322184606923401)
XLA Ops:
  6.5 0.7 all-gather.3.cloned.1.call-update
  7.3 0.7 all-gather.5.cloned.1.call-update
  8.1 0.4 multiply_reduce_fusion
  8.4 0.1 rsqrt.21
  8.5 0.1 iota_compare_fusion.2
  8.7 0.1 copy.37
  8.8 0.2 fusion.31
  9.0 0.1 fusion.33
  9.1 0.4 fusion.6
  9.5 69.6 %all-gather.3.cloned.1.call-done = bf16[3584,512]{1,0:T(8,128)(2,1)} async-done(((bf16[448,512]{1,0:T(8,128)(2,1)}), bf16[3584,512]{1,0:T(8,128)(2,1)}) %all-gather.3.cloned.1.call-update) | async-done | bytes 3670032 | tf_op jit(solution)/shard_map/all_gather | solution.py:41
  79.1 3.0 %fusion.21 = bf16[208,512]{1,0:T(8,128)(2,1)S(1)} fusion(bf16[3584,512]{1,0:T(8,128)(2,1)} %all-gather.3.cloned.1.call-done, bf16[192,3584]{1,0:T(8,128)(2,1)S(1)} %fusion.6, bf16[16,3584]{1,0:T(8,128)(2,1)S(1)} %fusion.33), kind=kOutput, calls=%fused_computation.29 | convolution fusion | flops 766451712 | bytes 5373952 | tf_op jit(solution)/shard_map/dot_general | solution.py:21
  82.1 5.3 %all_gather.21 = bf16[64,256]{1,0:T(8,128)(2,1)S(1)} all-gather(bf16[16,256]{1,0:T(8,128)(2,1)S(1)} %get-tuple-element.10), channel_id=1, replica_groups=mesh['grp'=4,'dev'=8] {'grp'}, dimensions={0}, use_global_device_ids=true | all-gather | bytes 40960 | tf_op jit(solution)/shard_map/all_gather | solution.py:51
  87.4 32.1 %all_gather.22 = bf16[512,256]{1,0:T(8,128)(2,1)S(1)} all-gather(bf16[64,256]{1,0:T(8,128)(2,1)S(1)} %all_gather.21), channel_id=1, replica_groups=mesh['grp'=4,'dev'=8] {'dev'}, dimensions={0}, use_global_device_ids=true | all-gather | bytes 294912 | tf_op jit(solution)/shard_map/all_gather | solution.py:55
  119.5 0.1 reshape.158
  119.6 5.2 %all_gather.19 = bf16[64,256]{1,0:T(8,128)(2,1)S(1)} all-gather(bf16[16,256]{1,0:T(8,128)(2,1)S(1)} %get-tuple-element.9), channel_id=1, replica_groups=mesh['grp'=4,'dev'=8] {'grp'}, dimensions={0}, use_global_device_ids=true | all-gather | bytes 40960 | tf_op jit(solution)/shard_map/all_gather | solution.py:52
  124.8 31.6 %all_gather.20 = bf16[512,256]{1,0:T(8,128)(2,1)S(1)} all-gather(bf16[64,256]{1,0:T(8,128)(2,1)S(1)} %all_gather.19), channel_id=1, replica_groups=mesh['grp'=4,'dev'=8] {'dev'}, dimensions={0}, use_global_device_ids=true | all-gather | bytes 294912 | tf_op jit(solution)/shard_map/all_gather | solution.py:58
  156.3 0.1 reshape.157
  156.5 106.9 %all-gather.5.cloned.1.call-done = bf16[3584,1792]{1,0:T(8,128)(2,1)} async-done(((bf16[448,1792]{1,0:T(8,128)(2,1)}), bf16[3584,1792]{1,0:T(8,128)(2,1)}) %all-gather.5.cloned.1.call-update) | async-done | bytes 12845072 | tf_op jit(solution)/shard_map/all_gather | solution.py:45
  263.4 7.3 %convolution_convert_fusion = bf16[192,1792]{1,0:T(8,128)(2,1)S(1)} fusion(bf16[192,3584]{1,0:T(8,128)(2,1)S(1)} %copy-done.3, bf16[3584,1792]{1,0:T(8,128)(2,1)} %all-gather.5.cloned.1.call-done), kind=kOutput, calls=%fused_computation.12 | convolution fusion | flops 2466594816 | bytes 14909440 | tf_op jit(solution)/shard_map/dot_general | solution.py:21
  270.7 0.8 reshape.159
  271.5 0.8 reshape.162
  272.3 3.3 %bitcast_reduce_fusion = (f32[192,2,7]{0,2,1:T(8,128)S(1)}, f32[2,512,192,7]{1,2,3,0:T(8,128)}) fusion(bf16[192,2,7,128]{3,2,1,0:T(8,128)(2,1)S(1)} %reshape.159, bf16[512,2,128,1]{2,1,0,3:T(2,128)(2,1)S(1)} %bitcast.46), kind=kOutput, calls=%fused_computation.1 | convolution fusion | flops 355071360 | bytes 6466048 | tf_op jit(solution)/shard_map/rhgd,nhd->rhgn/dot_general | solution.py:62
  275.6 0.1 reshape.171
  275.7 3.6 %fusion.1 = f32[192,2,7]{0,2,1:T(8,128)S(1)} fusion(f32[2,512,192,7]{1,2,3,0:T(8,128)} %get-tuple-element.12, f32[192,2,7]{0,2,1:T(8,128)S(1)} %broadcast_maximum_fusion), kind=kLoop, calls=%fused_computation.3 | loop fusion | flops 4126080 | bytes 5526528 | tf_op jit(solution)/shard_map/reduce_sum | solution.py:67
  279.3 0.6 copy-done
  279.9 1.3 fusion.3
  281.2 0.1 reshape.170
  281.2 0.7 fusion.41
  282.0 0.3 fusion.19
  282.3 1.3 fusion.18
  283.6 0.5 copy.47
  284.1 1.6 convert_element_type.47
  (28 shorter events, 0.2 us)
Async XLA Ops:
  6.5 1.5 copy-start.1
  6.5 72.6 %all-gather.3.cloned.1.call-start = ((), (), s32[]{:S(2)}) async-start(), calls=%async_computation | async-start | bytes 4128768 | tf_op jit(solution)/shard_map/all_gather | solution.py:41
  7.3 1.3 copy-start.7
  7.3 1.4 copy-start.5
  7.3 1.5 copy-start.4
  7.3 1.7 copy-start.6
  7.3 256.1 %all-gather.5.cloned.1.call-start = ((), (), s32[]{:S(2)}) async-start(), calls=%async_computation.1 | async-start | bytes 14450688 | tf_op jit(solution)/shard_map/all_gather | solution.py:45
  9.5 72.6 %copy-start.2 = (bf16[192,3584]{1,0:T(8,128)(2,1)}, bf16[192,3584]{1,0:T(8,128)(2,1)S(1)}, u32[]{:S(2)}) copy-start(bf16[192,3584]{1,0:T(8,128)(2,1)S(1)} %fusion.6) | copy-start | bytes 4128772
  82.1 181.3 %copy-start.3 = (bf16[192,3584]{1,0:T(8,128)(2,1)S(1)}, bf16[192,3584]{1,0:T(8,128)(2,1)}, u32[]{:S(2)}) copy-start(bf16[192,3584]{1,0:T(8,128)(2,1)} %copy-done.2) | copy-start | bytes 4128772
  275.7 4.2 %copy-start = (f32[2,512,192,7]{1,2,3,0:T(8,128)S(1)}, f32[2,512,192,7]{1,2,3,0:T(8,128)}, u32[]{:S(2)}) copy-start(f32[2,512,192,7]{1,2,3,0:T(8,128)} %get-tuple-element.12) | copy-start | bytes 16515076
Sparse Core Ops, SparseCore 0:
  9.5 69.5 all-gather.2
  81.3 182.1 all-gather.4
where the time goes:
time: 293 us
  waiting for transfers between devices  178 us (61%)
  blocking collectives  74.2 us (25%)
  matrix products  16.8 us (6%)
  between operations  13.6 us (5%)
  other arithmetic  5.11 us (2%)
  local copies, waits for them, and re-layouts  4.79 us (2%)
    all_gather x1, waiting for transfers between devices, local(): lax.all_gather(w_query, 'dev', axis=0, tiled=True)  107 us
    all_gather x1, waiting for transfers between devices, local(): lax.all_gather(w_keyval, 'dev', axis=0, tiled=True)  69.6 us
    all_gather x1, blocking collectives, local(): lax.all_gather(context_keys, 'dev', axis=0, tiled=True)  32.1 us
    all_gather x1, blocking collectives, local(): lax.all_gather(context_values, 'dev', axis=0, tiled=True)  31.6 us
    dot_general x2, matrix products, projector(): return jnp.dot(source, incoming, preferred_element_type=jnp.float32)  10.3 us
  transfers between devices with their start and end apart: 2, of which 2 were waited for; matrix products, arithmetic and copies ran while one was open for 2% of the time, Pallas kernels for 0%

commit v1 on v0

v1 whole, which is shorter than its diff:
```python
import functools
import math

import jax
import jax.numpy as jnp
from jax import lax
from jax.experimental import pallas as pl
from jax.experimental.pallas import tpu as pltpu
from jax.sharding import PartitionSpec as P

HEAD_SIZE = 128
KEYVAL_HEADS = 2
NEG_FILL = -1e30
MESH = pl.DeviceIdType.MESH


def split_heads(head_groups):
    widths = []
    while head_groups > 0:
        widths.append(min(2, head_groups))
        head_groups -= widths[-1]
    return widths


def norm_rows(src, dst, gain_ref, count, first, block=64):
    def body(i, carry):
        rows = pl.ds(pl.multiple_of(first + i * block, block), block)
        widened = src[rows, :].astype(jnp.float32)
        inverse = lax.rsqrt(jnp.mean(widened * widened, axis=-1, keepdims=True) + 1e-06)
        dst[rows, :] = (widened * inverse * gain_ref[...]).astype(jnp.bfloat16)
        return carry

    lax.fori_loop(0, count // block, body, 0)


def kernel(
    n_dev, samples, slots, widths, ctx_ref, step_ref, gain_ref, wq_ref, wkv_ref, lens_ref, mask_ref,
    out_ref, rows_buf, ctx_buf, wkv_buf, *rest
):
    groups = len(widths)
    wq_bufs = rest[:groups]
    (ckv_buf, skv_buf, q_buf, aux_buf, part_buf,
     recv_sem, send_sem, local_sem, pair_recv, out_recv) = rest[groups:]
    own_rows = samples * slots
    shard = wkv_ref.shape[0]
    ctx_rows = ctx_ref.shape[0]
    half_cols = sum(widths) * HEAD_SIZE
    line = n_dev // 2

    g = lax.axis_index("grp")
    d = lax.axis_index("dev")
    core = lax.rem(g, 2)
    head = lax.rem(g // 2, 2)
    a = d // 2
    b = lax.rem(d, 2)
    sibling = (g + 1 - 2 * core, d)
    pair = (g + 2 - 4 * head, d)
    across = (g, 2 * a + 1 - b)

    def along(t):
        return 2 * lax.rem(a + t, line) + b

    barrier = pltpu.get_barrier_semaphore()
    friends = [sibling, pair, across] + [(g, along(t)) for t in range(1, line)]
    for friend in friends:
        pl.semaphore_signal(barrier, inc=1, device_id=friend, device_id_type=MESH)
    pl.semaphore_wait(barrier, len(friends))

    pending = []

    def send(src, dst, sem, target):
        copy = pltpu.make_async_remote_copy(
            src_ref=src, dst_ref=dst, send_sem=send_sem.at[len(pending)], recv_sem=sem,
            device_id=target, device_id_type=MESH,
        )
        copy.start()
        pending.append(copy)

    class Gather:
        def __init__(self, kind, buf, size):
            self.kind, self.buf, self.size = kind, buf, size
            self.halves = 2 if size % 32 == 0 else 1
            self.piece = size // self.halves
            self.mine = core if self.halves == 2 else 0

        def at(self, src, half):
            start = src * self.size + half * self.piece
            return self.buf.at[pl.ds(pl.multiple_of(start, 16), self.piece)]

        def sem(self, src, half):
            return recv_sem.at[self.kind, half, src]

        def wait(self, src, half):
            ref = self.at(src, half)
            pltpu.make_async_copy(ref, ref, self.sem(src, half)).wait()

        def forward(self, src, target):
            ref = self.at(src, self.mine)
            send(ref, ref, self.sem(src, self.mine), target)

        def start(self, sources):
            for target in [(g, along(t)) for t in range(1, line)] + [across]:
                send(sources, self.at(d, self.mine), self.sem(d, self.mine), target)

        def along_line(self):
            for t in range(1, line):
                src = along(t)
                self.wait(src, self.mine)
                self.forward(src, across)
                if self.halves == 2:
                    self.forward(src, sibling)

        def across_line(self):
            for t in range(line):
                src = 2 * lax.rem(a + t, line) + 1 - b
                self.wait(src, self.mine)
                if self.halves == 2:
                    self.forward(src, sibling)

        def finish(self):
            if self.halves == 2:
                for t in range(1, n_dev):
                    self.wait(lax.rem(d + t, n_dev), 1 - self.mine)

    send(step_ref, rows_buf.at[pl.ds(0, own_rows)], pair_recv.at[0], pair)

    gathers = [Gather(0, wkv_buf, shard)]
    gathers += [Gather(1 + i, wq_bufs[i], shard) for i in range(groups)]
    ctx_gather = Gather(1 + groups, ckv_buf, ctx_rows)

    locals_ = []

    def local(src, dst):
        copy = pltpu.make_async_copy(src, dst, local_sem.at[len(locals_)])
        copy.start()
        locals_.append(copy)

    own_shard = pl.ds(pl.multiple_of(d * shard, 16), shard)
    for part in range(2):
        cols = pl.ds(pl.multiple_of((part * KEYVAL_HEADS + head) * HEAD_SIZE, HEAD_SIZE), HEAD_SIZE)
        local(wkv_ref.at[:, cols], wkv_buf.at[own_shard, pl.ds(part * HEAD_SIZE, HEAD_SIZE)])
    local(step_ref, rows_buf.at[pl.ds(own_rows, own_rows)])
    col = 0
    starts = []
    for i in range(groups):
        width = widths[i] * HEAD_SIZE
        cols = pl.ds(pl.multiple_of(head * half_cols + col, HEAD_SIZE), width)
        local(wq_ref.at[:, cols], wq_bufs[i].at[own_shard])
        starts.append(cols)
        col += width
    locals_[0].wait()
    locals_[1].wait()
    gathers[0].start(gathers[0].at(d, gathers[0].mine))
    for i in range(groups):
        gather = gathers[1 + i]
        first = pl.multiple_of(gather.mine * gather.piece, 16)
        gather.start(wq_ref.at[pl.ds(first, gather.piece), starts[i]])

    t_at = lax.broadcasted_iota(jnp.int32, (slots, slots), 0)
    u_at = lax.broadcasted_iota(jnp.int32, (slots, slots), 1)
    for s in range(samples):
        length = lens_ref[s]
        allowed = (u_at <= t_at) & ((u_at == t_at) | (mask_ref[s] == 1)) & (u_at < length)
        rows = pl.ds(own_rows + s * slots, slots)
        aux_buf[rows, 0:slots] = jnp.where(allowed, 1.0, 0.0).astype(jnp.bfloat16)
        aux_buf[rows, slots:2 * slots] = jnp.where(t_at < length, 1.0, 0.0).astype(jnp.bfloat16)
    send(aux_buf.at[pl.ds(own_rows, own_rows)], aux_buf.at[pl.ds(0, own_rows)], pair_recv.at[1], pair)

    norm_rows(ctx_ref, ctx_buf, gain_ref, ctx_rows, 0)
    gathers[0].along_line()
    locals_[2].wait()
    norm_rows(rows_buf, rows_buf, gain_ref, own_rows, own_rows)
    gathers[0].across_line()
    gathers[1].along_line()
    gathers[0].finish()
    own_ckv = jnp.dot(ctx_buf[...], wkv_buf[...], preferred_element_type=jnp.float32)
    ckv_buf[pl.ds(pl.multiple_of(d * ctx_rows, 16), ctx_rows), :] = own_ckv.astype(jnp.bfloat16)
    ctx_gather.start(ctx_gather.at(d, ctx_gather.mine))
    gathers[1].across_line()
    ctx_gather.along_line()
    ctx_gather.across_line()

    for i in range(2):
        ref = (rows_buf, aux_buf)[i].at[pl.ds(0, own_rows)]
        pltpu.make_async_copy(ref, ref, pair_recv.at[i]).wait()
    norm_rows(rows_buf, rows_buf, gain_ref, own_rows, 0)
    skv_buf[...] = jnp.dot(
        rows_buf[...], wkv_buf[...], preferred_element_type=jnp.float32
    ).astype(jnp.bfloat16)
    ctx_gather.finish()

    score_scale = 1.0 / math.sqrt(HEAD_SIZE)
    contract_last = (((1,), (1,)), ((), ()))

    def attend(heads, sample):
        rows = pl.ds(pl.multiple_of(sample * slots, slots), slots)
        q = q_buf[0:heads, rows, :].reshape(heads * slots, HEAD_SIZE)
        ctx_scores = lax.dot_general(
            q, ckv_buf[:, 0:HEAD_SIZE], contract_last, preferred_element_type=jnp.float32
        ) * score_scale
        step_scores = lax.dot_general(
            q, skv_buf[rows, 0:HEAD_SIZE], contract_last, preferred_element_type=jnp.float32
        ) * score_scale
        allowed = aux_buf[rows, 0:slots].astype(jnp.float32) > 0.5
        step_scores = jnp.where(
            allowed[None], step_scores.reshape(heads, slots, slots), NEG_FILL
        ).reshape(heads * slots, slots)
        top = jnp.maximum(
            jnp.max(ctx_scores, axis=-1, keepdims=True), jnp.max(step_scores, axis=-1, keepdims=True)
        )
        ctx_weights = jnp.exp(ctx_scores - top)
        step_weights = jnp.exp(step_scores - top)
        weight_sum = jnp.sum(ctx_weights, axis=-1, keepdims=True)
        weight_sum += jnp.sum(step_weights, axis=-1, keepdims=True)
        attended = jnp.dot(
            ctx_weights.astype(jnp.bfloat16), ckv_buf[:, HEAD_SIZE:], preferred_element_type=jnp.float32
        )
        attended += jnp.dot(
            step_weights.astype(jnp.bfloat16), skv_buf[rows, HEAD_SIZE:], preferred_element_type=jnp.float32
        )
        attended = (attended / weight_sum).reshape(heads, slots, HEAD_SIZE)
        live = aux_buf[rows, slots:slots + 1].astype(jnp.float32) > 0.5
        return jnp.where(live[None], attended, 0.0).astype(jnp.bfloat16)

    col = 0
    for i in range(groups):
        heads = widths[i]
        if i + 1 < groups:
            gathers[2 + i].along_line()
        locals_[3 + i].wait()
        gathers[1 + i].finish()
        q = jnp.dot(rows_buf[...], wq_bufs[i][...], preferred_element_type=jnp.float32)
        for h in range(heads):
            q_buf[h] = q[:, h * HEAD_SIZE:(h + 1) * HEAD_SIZE].astype(jnp.bfloat16)

        def for_pair(sample, carry, heads=heads, col=col):
            attended = attend(heads, sample)
            rows = pl.ds(pl.multiple_of(sample * slots, slots), slots)
            for h in range(heads):
                part_buf[rows, col + h * HEAD_SIZE:col + (h + 1) * HEAD_SIZE] = attended[h]
            return carry

        def for_own(sample, carry, heads=heads, col=col):
            attended = attend(heads, samples + sample)
            rows = pl.ds(pl.multiple_of(sample * slots, slots), slots)
            for h in range(heads):
                first = pl.multiple_of(head * half_cols + col + h * HEAD_SIZE, HEAD_SIZE)
                out_ref[rows, pl.ds(first, HEAD_SIZE)] = attended[h]
            return carry

        lax.fori_loop(0, samples, for_pair, 0)
        width = heads * HEAD_SIZE
        there = out_ref.at[:, pl.ds(pl.multiple_of(head * half_cols + col, HEAD_SIZE), width)]
        send(part_buf.at[:, pl.ds(col, width)], there, out_recv.at[i], pair)
        lax.fori_loop(0, samples, for_own, 0)
        col += width
        if i + 1 < groups:
            gathers[2 + i].across_line()

    col = 0
    for i in range(groups):
        width = widths[i] * HEAD_SIZE
        here = out_ref.at[:, pl.ds(pl.multiple_of((1 - head) * half_cols + col, HEAD_SIZE), width)]
        pltpu.make_async_copy(here, here, out_recv.at[i]).wait()
        col += width
    for copy in pending:
        copy.wait_send()


def local(ctx_hidden, step_hidden, norm_gain, w_query, w_keyval, step_lengths, step_mask, n_dev):
    samples, slots, features = step_hidden.shape
    own_rows = samples * slots
    query_cols = w_query.shape[1]
    widths = split_heads(query_cols // HEAD_SIZE // KEYVAL_HEADS)
    groups = len(widths)
    ctx_rows = ctx_hidden.shape[0]
    bf16 = jnp.bfloat16
    sends = (groups + 2) * (2 * n_dev) + 2 + groups
    vmem = pl.BlockSpec(memory_space=pltpu.VMEM)
    smem = pl.BlockSpec(memory_space=pltpu.SMEM)
    anywhere = pl.BlockSpec(memory_space=pl.ANY)
    out = pl.pallas_call(
        functools.partial(kernel, n_dev, samples, slots, widths),
        out_shape=jax.ShapeDtypeStruct((own_rows, query_cols), bf16),
        in_specs=[vmem, anywhere, vmem, anywhere, anywhere, smem, vmem],
        out_specs=vmem,
        scratch_shapes=[
            pltpu.VMEM((2 * own_rows, features), bf16),
            pltpu.VMEM((ctx_rows, features), bf16),
            pltpu.VMEM((features, 2 * HEAD_SIZE), bf16),
        ]
        + [pltpu.VMEM((features, width * HEAD_SIZE), bf16) for width in widths]
        + [
            pltpu.VMEM((n_dev * ctx_rows, 2 * HEAD_SIZE), bf16),
            pltpu.VMEM((2 * own_rows, 2 * HEAD_SIZE), bf16),
            pltpu.VMEM((max(widths), 2 * own_rows, HEAD_SIZE), bf16),
            pltpu.VMEM((2 * own_rows, 2 * slots), bf16),
            pltpu.VMEM((own_rows, query_cols // 2), bf16),
            pltpu.SemaphoreType.DMA((groups + 2, 2, n_dev)),
            pltpu.SemaphoreType.DMA((sends,)),
            pltpu.SemaphoreType.DMA((3 + groups,)),
            pltpu.SemaphoreType.DMA((2,)),
            pltpu.SemaphoreType.DMA((groups,)),
        ],
        compiler_params=pltpu.CompilerParams(
            collective_id=0, has_side_effects=True, vmem_limit_bytes=48 * 1024 * 1024
        ),
        name="shared_context_attention",
    )(
        ctx_hidden, step_hidden.reshape(own_rows, features), norm_gain.reshape(1, features),
        w_query, w_keyval, step_lengths, step_mask,
    )
    return out.reshape(samples, slots, query_cols)


def solution(mesh):
    placed = (
        P("dev", None),
        P(("grp", "dev"), None, None),
        P(),
        P("dev", None),
        P("dev", None),
        P(("grp", "dev")),
        P(("grp", "dev"), None, None),
    )
    return jax.shard_map(
        functools.partial(local, n_dev=mesh.shape["dev"]),
        mesh=mesh, in_specs=placed, out_specs=P(("grp", "dev"), None, None), check_vma=False,
    )
```

time: 293 us -> 96.3 us (0.33)
  waiting for transfers between devices: 178 us -> 0 us
  Pallas kernels: 0 us -> 88 us
  blocking collectives: 74.2 us -> 0 us
  matrix products: 16.8 us -> 0 us
  between operations: 13.6 us -> 0.03 us
  other arithmetic: 5.11 us -> 0 us
  local copies, waits for them, and re-layouts: 4.79 us -> 7.91 us
    all_gather x2 -> x0, waiting for transfers between devices: 177 us -> none  [the longest x1 107 us: local(): lax.all_gather(w_query, 'dev', axis=0, tiled=True)]
    pallas_call x0 -> x1, Pallas kernels: none -> 88 us  [local(): pl.pallas_call(functools.partial(kernel, n_dev, samples, slots, widths),...]
    all_gather x4 -> x0, blocking collectives: 74.2 us -> none  [the longest x1 32.1 us: local(): lax.all_gather(context_keys, 'dev', axis=0, tiled=True)]
    dot_general x6 -> x0, matrix products: 16.8 us -> none  [the longest x2 10.3 us: projector(): return jnp.dot(source, incoming, preferred_element_type=jnp.float32)]
    unnamed x16 -> x13, local copies, waits for them, and re-layouts: 0.6 us -> 7.19 us
    reduce_sum x4 -> x0, other arithmetic: 4.46 us -> none  [the longest x1 3.63 us: local(): weight_sum = weights.sum(-1)]
  transfers between devices with their start and end apart: 2 -> 0, of which waited for: 2 -> 0; matrix products, arithmetic and copies ran while one was open for 2% -> 0% of each run, Pallas kernels for 0% -> 0%
where the time goes in v1:
time: 96.3 us; the launch traced here: 96 us
  Pallas kernels  88 us (91%)
  local copies, waits for them, and re-layouts  7.91 us (8%)
    pallas_call x1, Pallas kernels, local(): pl.pallas_call(functools.partial(kernel, n_dev, samples, slots, widths),...  88 us
    unnamed x13, local copies, waits for them, and re-layouts  7.19 us

profile of v1, /device:TPU:0, one launch (start us, length us, event | category | flops | bytes accessed | tf_op | source)
XLA Modules:
  0.0 96.0 jit_solution(6968565049687582327)
XLA Ops:
  0.0 0.7 reshape.10.gain_ref
  0.7 0.0 copy-start
  0.7 1.4 %copy-done = bf16[448,1792]{1,0:T(8,128)(2,1)S(1)} copy-done((bf16[448,1792]{1,0:T(8,128)(2,1)S(1)}, bf16[448,1792]{1,0:T(8,128)(2,1)}, u32[]{:S(2)}) %copy-start) | copy-done | bytes 1605656
  2.2 0.0 copy-start.1
  2.2 1.3 %copy-done.1 = bf16[3,64,3584]{2,1,0:T(8,128)(2,1)S(1)} copy-done((bf16[3,64,3584]{2,1,0:T(8,128)(2,1)S(1)}, bf16[3,64,3584]{2,1,0:T(8,128)(2,1)}, u32[]{:S(2)}) %copy-start.1) | copy-done | bytes 1376280
  3.5 0.0 copy-start.2
  3.5 1.0 %copy-done.2 = bf16[64,3584]{1,0:T(8,128)(2,1)S(1)} copy-done((bf16[64,3584]{1,0:T(8,128)(2,1)S(1)}, bf16[64,3584]{1,0:T(8,128)(2,1)}, u32[]{:S(2)}) %copy-start.2) | copy-done | bytes 458776
  4.5 0.0 copy-start.3
  4.5 1.0 %copy-done.3 = bf16[448,512]{1,0:T(8,128)(2,1)S(1)} copy-done((bf16[448,512]{1,0:T(8,128)(2,1)S(1)}, bf16[448,512]{1,0:T(8,128)(2,1)}, u32[]{:S(2)}) %copy-start.3) | copy-done | bytes 458776
  5.5 0.0 copy-start.4
  5.5 0.9 copy-done.4
  6.4 0.0 copy-start.5
  6.4 0.7 copy-done.5
  7.1 88.0 %shared_context_attention.1 = bf16[192,1792]{1,0:T(8,128)(2,1)S(1)} custom-call(bf16[64,3584]{1,0:T(8,128)(2,1)S(1)} %copy-done.2, bf16[192,3584]{1,0:T(8,128)(2,1)S(1)} %bitcast.3, f32[1,3584]{1,0:T(1,128)S(1)} %reshape.10.gain_ref, bf16[448,1792]{1,0:T(8,128)(2,1)S(1)} %copy-done, bf16[448,512]{1,0:T(8,128)(2,1)S(1)} %copy-done.3, s32[3]{0:T(128)S(1)} %copy-done.5, ...), custom_call_target="tpu_custom_call" | custom-call | tf_op jit(solution)/shard_map/shared_context_attention/pallas_call | solution.py:282
  95.1 0.8 copy.9
Async XLA Ops:
  0.7 1.4 %copy-start = (bf16[448,1792]{1,0:T(8,128)(2,1)S(1)}, bf16[448,1792]{1,0:T(8,128)(2,1)}, u32[]{:S(2)}) copy-start(bf16[448,1792]{1,0:T(8,128)(2,1)} %wq_ref.1) | copy-start | bytes 4816900
  2.2 1.3 %copy-start.1 = (bf16[3,64,3584]{2,1,0:T(8,128)(2,1)S(1)}, bf16[3,64,3584]{2,1,0:T(8,128)(2,1)}, u32[]{:S(2)}) copy-start(bf16[3,64,3584]{2,1,0:T(8,128)(2,1)} %param.8) | copy-start | bytes 4128772
  3.5 1.0 %copy-start.2 = (bf16[64,3584]{1,0:T(8,128)(2,1)S(1)}, bf16[64,3584]{1,0:T(8,128)(2,1)}, u32[]{:S(2)}) copy-start(bf16[64,3584]{1,0:T(8,128)(2,1)} %ctx_ref.1) | copy-start | bytes 1376260
  4.5 1.0 %copy-start.3 = (bf16[448,512]{1,0:T(8,128)(2,1)S(1)}, bf16[448,512]{1,0:T(8,128)(2,1)}, u32[]{:S(2)}) copy-start(bf16[448,512]{1,0:T(8,128)(2,1)} %wkv_ref.1) | copy-start | bytes 1376260
  5.5 0.9 copy-start.4
  6.4 0.7 copy-start.5

commit v2 on v1

v2 whole, which is shorter than its diff:
```python
import functools
import math

import jax
import jax.numpy as jnp
from jax import lax
from jax.experimental import pallas as pl
from jax.experimental.pallas import tpu as pltpu
from jax.sharding import PartitionSpec as P

HEAD_SIZE = 128
SLAB = 16
KEYVAL_HEADS = 2
NEG_FILL = -1e30
MESH = pl.DeviceIdType.MESH


def split_heads(head_groups):
    widths = []
    while head_groups > 0:
        widths.append(min(2, head_groups))
        head_groups -= widths[-1]
    return widths


def norm_rows(src, dst, gain_ref, count, first, block=64):
    def body(i, carry):
        rows = pl.ds(pl.multiple_of(first + i * block, block), block)
        widened = src[rows, :].astype(jnp.float32)
        inverse = lax.rsqrt(jnp.mean(widened * widened, axis=-1, keepdims=True) + 1e-06)
        dst[rows, :] = (widened * inverse * gain_ref[...]).astype(jnp.bfloat16)
        return carry

    lax.fori_loop(0, count // block, body, 0)


def kernel(
    n_dev, samples, slots, widths, ctx_hbm, step_ref, gain_hbm, wq_ref, wkv_ref, lens_ref, mask_hbm,
    out_ref, ctx_ref, gain_tiles, gain_ref, mask_ref, rows_buf, ctx_buf, wkv_buf, *rest
):
    groups = len(widths)
    wq_bufs = rest[:groups]
    (ckv_buf, keyval_buf, q_buf, aux_buf, may_buf, part_buf,
     recv_sem, send_sem, local_sem, pair_recv, out_recv) = rest[groups:]
    own_rows = samples * slots
    shard = wkv_ref.shape[0]
    ctx_rows = ctx_ref.shape[0]
    half_cols = sum(widths) * HEAD_SIZE
    line = n_dev // 2

    g = lax.axis_index("grp")
    d = lax.axis_index("dev")
    core = lax.rem(g, 2)
    head = lax.rem(g // 2, 2)
    a = d // 2
    b = lax.rem(d, 2)
    sibling = (g + 1 - 2 * core, d)
    pair = (g + 2 - 4 * head, d)
    across = (g, 2 * a + 1 - b)

    def along(t):
        return 2 * lax.rem(a + t, line) + b

    barrier = pltpu.get_barrier_semaphore()
    friends = [sibling, pair, across] + [(g, along(t)) for t in range(1, line)]
    for friend in friends:
        pl.semaphore_signal(barrier, inc=1, device_id=friend, device_id_type=MESH)
    pl.semaphore_wait(barrier, len(friends))

    pending = []

    def send(src, dst, sem, target):
        copy = pltpu.make_async_remote_copy(
            src_ref=src, dst_ref=dst, send_sem=send_sem.at[len(pending)], recv_sem=sem,
            device_id=target, device_id_type=MESH,
        )
        copy.start()
        pending.append(copy)

    class Gather:
        def __init__(self, kind, buf, size):
            self.kind, self.buf, self.size = kind, buf, size
            self.halves = 2 if size % 32 == 0 else 1
            self.piece = size // self.halves
            self.mine = core if self.halves == 2 else 0

        def at(self, src, half):
            start = src * self.size + half * self.piece
            return self.buf.at[pl.ds(pl.multiple_of(start, 16), self.piece)]

        def sem(self, src, half):
            return recv_sem.at[self.kind, half, src]

        def wait(self, src, half):
            ref = self.at(src, half)
            pltpu.make_async_copy(ref, ref, self.sem(src, half)).wait()

        def forward(self, src, target):
            ref = self.at(src, self.mine)
            send(ref, ref, self.sem(src, self.mine), target)

        def starts(self, source):
            targets = [(g, along(t)) for t in range(1, line)]
            targets.insert(1, across)
            place, sem = self.at(d, self.mine), self.sem(d, self.mine)
            return [functools.partial(send, source, place, sem, target) for target in targets]

        def relay_along(self, t):
            src = along(t)
            self.wait(src, self.mine)
            self.forward(src, across)
            if self.halves == 2:
                self.forward(src, sibling)

        def relay_across(self, t):
            src = 2 * lax.rem(a + t, line) + 1 - b
            self.wait(src, self.mine)
            if self.halves == 2:
                self.forward(src, sibling)

        def along_line(self):
            return [functools.partial(self.relay_along, t) for t in range(1, line)]

        def across_line(self):
            return [functools.partial(self.relay_across, t) for t in range(line)]

        def finish(self):
            if self.halves == 2:
                for t in range(1, n_dev):
                    self.wait(lax.rem(d + t, n_dev), 1 - self.mine)

    slabs = own_rows // SLAB

    def send_slab(i):
        rows = pl.ds(i * SLAB, SLAB)
        send(step_ref.at[rows], rows_buf.at[rows], pair_recv.at[i], pair)

    def run(*lists):
        lists = [list(events) for events in lists]
        while any(lists):
            for events in lists:
                if events:
                    events.pop(0)()

    gathers = [Gather(0, wkv_buf, shard)]
    gathers += [Gather(1 + i, wq_bufs[i], shard) for i in range(groups)]
    ctx_gather = Gather(1 + groups, ckv_buf, ctx_rows)

    locals_ = []

    def local(src, dst):
        copy = pltpu.make_async_copy(src, dst, local_sem.at[len(locals_)])
        copy.start()
        locals_.append(copy)

    own_shard = pl.ds(pl.multiple_of(d * shard, 16), shard)
    for part in range(2):
        cols = pl.ds(pl.multiple_of((part * KEYVAL_HEADS + head) * HEAD_SIZE, HEAD_SIZE), HEAD_SIZE)
        local(wkv_ref.at[:, cols], wkv_buf.at[own_shard, pl.ds(part * HEAD_SIZE, HEAD_SIZE)])
    local(step_ref, rows_buf.at[pl.ds(own_rows, own_rows)])
    small = [(ctx_hbm, ctx_ref), (gain_hbm, gain_tiles), (mask_hbm, mask_ref)]
    for src, dst in small:
        local(src, dst)
    col = 0
    starts = []
    for i in range(groups):
        width = widths[i] * HEAD_SIZE
        cols = pl.ds(pl.multiple_of(head * half_cols + col, HEAD_SIZE), width)
        local(wq_ref.at[:, cols], wq_bufs[i].at[own_shard])
        starts.append(cols)
        col += width
    locals_[0].wait()
    locals_[1].wait()
    pushes = []
    for i in range(groups):
        gather = gathers[1 + i]
        first = pl.multiple_of(gather.mine * gather.piece, 16)
        pushes.append(gather.starts(wq_ref.at[pl.ds(first, gather.piece), starts[i]]))
    pair_sends = [functools.partial(send_slab, i) for i in range(slabs)]
    third = -(-slabs // 3)
    run(gathers[0].starts(gathers[0].at(d, gathers[0].mine)) + pushes[0], pair_sends[:third])

    t_at = lax.broadcasted_iota(jnp.int32, (slots, slots), 0)
    u_at = lax.broadcasted_iota(jnp.int32, (slots, slots), 1)
    for copy in locals_[3:6]:
        copy.wait()
    for i in range(gain_tiles.shape[0]):
        gain_ref[:, i * HEAD_SIZE:(i + 1) * HEAD_SIZE] = gain_tiles[i:i + 1, :]
    for s in range(samples):
        length = lens_ref[s]
        allowed = (u_at <= t_at) & ((u_at == t_at) | (mask_ref[s] == 1)) & (u_at < length)
        rows = pl.ds(own_rows + s * slots, slots)
        aux_buf[rows, 0:slots] = jnp.where(allowed, 1.0, 0.0).astype(jnp.bfloat16)
        aux_buf[rows, slots:2 * slots] = jnp.where(t_at < length, 1.0, 0.0).astype(jnp.bfloat16)
    send(aux_buf.at[pl.ds(own_rows, own_rows)], aux_buf.at[pl.ds(0, own_rows)], pair_recv.at[slabs], pair)

    def expand(group):
        for s in range(samples):
            at = slice(s * slots, (s + 1) * slots)
            rows = slice(group * own_rows + s * slots, group * own_rows + (s + 1) * slots)
            may_buf[rows, at] = aux_buf[rows, 0:slots].astype(jnp.float32)

    all_ctx = n_dev * ctx_rows

    def project_step(group):
        rows = pl.ds(group * own_rows, own_rows)
        keyval_buf[group, pl.ds(all_ctx, own_rows), :] = jnp.dot(
            rows_buf[rows, :], wkv_buf[...], preferred_element_type=jnp.float32
        ).astype(jnp.bfloat16)

    def project_query(i, first, count):
        rows = pl.ds(first, count)
        q = jnp.dot(rows_buf[rows, :], wq_bufs[i][...], preferred_element_type=jnp.float32)
        for h in range(widths[i]):
            q_buf[h, rows, :] = q[:, h * HEAD_SIZE:(h + 1) * HEAD_SIZE].astype(jnp.bfloat16)

    score_scale = 1.0 / math.sqrt(HEAD_SIZE)
    contract_last = (((1,), (1,)), ((), ()))
    firsts = [sum(widths[:i]) * HEAD_SIZE for i in range(groups)]

    def attend(i, group):
        heads = widths[i]
        rows = pl.ds(group * own_rows, own_rows)
        q = q_buf[0:heads, rows, :].reshape(heads * own_rows, HEAD_SIZE)
        scores = lax.dot_general(
            q, keyval_buf[group, :, 0:HEAD_SIZE], contract_last, preferred_element_type=jnp.float32
        ) * score_scale
        may = may_buf[rows, :] > 0.5
        step_scores = scores[:, all_ctx:].reshape(heads, own_rows, own_rows)
        step_scores = jnp.where(may[None], step_scores, NEG_FILL).reshape(heads * own_rows, own_rows)
        ctx_scores = scores[:, 0:all_ctx]
        top = jnp.maximum(
            jnp.max(ctx_scores, axis=-1, keepdims=True), jnp.max(step_scores, axis=-1, keepdims=True)
        )
        ctx_weights = jnp.exp(ctx_scores - top)
        step_weights = jnp.exp(step_scores - top)
        weight_sum = jnp.sum(ctx_weights, axis=-1, keepdims=True)
        weight_sum += jnp.sum(step_weights, axis=-1, keepdims=True)
        attended = jnp.dot(
            ctx_weights.astype(jnp.bfloat16), keyval_buf[group, pl.ds(0, all_ctx), HEAD_SIZE:],
            preferred_element_type=jnp.float32,
        )
        attended += jnp.dot(
            step_weights.astype(jnp.bfloat16), keyval_buf[group, pl.ds(all_ctx, own_rows), HEAD_SIZE:],
            preferred_element_type=jnp.float32,
        )
        attended = (attended / weight_sum).reshape(heads, own_rows, HEAD_SIZE)
        live = aux_buf[rows, slots:slots + 1].astype(jnp.float32) > 0.5
        attended = jnp.where(live[None], attended, 0.0).astype(jnp.bfloat16)
        for h in range(heads):
            col = firsts[i] + h * HEAD_SIZE
            if group == 0:
                part_buf[:, col:col + HEAD_SIZE] = attended[h]
            else:
                first = pl.multiple_of(head * half_cols + col, HEAD_SIZE)
                out_ref[:, pl.ds(first, HEAD_SIZE)] = attended[h]
        if group == 0:
            width = heads * HEAD_SIZE
            first = pl.multiple_of(head * half_cols + firsts[i], HEAD_SIZE)
            here = part_buf.at[:, pl.ds(firsts[i], width)]
            send(here, out_ref.at[:, pl.ds(first, width)], out_recv.at[i], pair)

    may_buf[...] = jnp.zeros_like(may_buf)
    expand(1)
    norm_rows(ctx_ref, ctx_buf, gain_ref, ctx_rows, 0)
    run(gathers[0].along_line(), pushes[1], pair_sends[third:2 * third])
    locals_[2].wait()
    norm_rows(rows_buf, rows_buf, gain_ref, own_rows, own_rows)
    run(gathers[0].across_line(), gathers[1].along_line(), pushes[2], pair_sends[2 * third:])
    gathers[0].finish()
    own_ckv = jnp.dot(ctx_buf[...], wkv_buf[...], preferred_element_type=jnp.float32)
    ckv_buf[pl.ds(pl.multiple_of(d * ctx_rows, 16), ctx_rows), :] = own_ckv.astype(jnp.bfloat16)
    run(ctx_gather.starts(ctx_gather.at(d, ctx_gather.mine)))
    project_step(1)
    run(gathers[1].across_line(), ctx_gather.along_line(), gathers[2].along_line(), sum(pushes[3:], []))
    run(ctx_gather.across_line())
    ctx_gather.finish()
    for group in range(2):
        keyval_buf[group, pl.ds(0, all_ctx), :] = ckv_buf[...]

    locals_[6].wait()
    gathers[1].finish()
    project_query(0, own_rows, own_rows)
    attend(0, 1)
    run(gathers[2].across_line(), gathers[3].along_line() if groups > 2 else [])
    for i in range(slabs):
        ref = rows_buf.at[pl.ds(i * SLAB, SLAB)]
        pltpu.make_async_copy(ref, ref, pair_recv.at[i]).wait()
    ref = aux_buf.at[pl.ds(0, own_rows)]
    pltpu.make_async_copy(ref, ref, pair_recv.at[slabs]).wait()
    norm_rows(rows_buf, rows_buf, gain_ref, own_rows, 0)
    expand(0)
    project_step(0)
    project_query(0, 0, own_rows)
    attend(0, 0)

    for i in range(1, groups):
        across_next = gathers[2 + i].across_line() if i + 1 < groups else []
        along_next = gathers[3 + i].along_line() if i + 2 < groups else []
        locals_[6 + i].wait()
        gathers[1 + i].finish()
        project_query(i, 0, 2 * own_rows)
        run(across_next[:2], along_next[:2])
        attend(i, 0)
        run(across_next[2:], along_next[2:])
        attend(i, 1)

    col = 0
    for i in range(groups):
        width = widths[i] * HEAD_SIZE
        here = out_ref.at[:, pl.ds(pl.multiple_of((1 - head) * half_cols + col, HEAD_SIZE), width)]
        pltpu.make_async_copy(here, here, out_recv.at[i]).wait()
        col += width
    for copy in pending:
        copy.wait_send()


def local(ctx_hidden, step_hidden, norm_gain, w_query, w_keyval, step_lengths, step_mask, n_dev):
    samples, slots, features = step_hidden.shape
    own_rows = samples * slots
    query_cols = w_query.shape[1]
    widths = split_heads(query_cols // HEAD_SIZE // KEYVAL_HEADS)
    groups = len(widths)
    ctx_rows = ctx_hidden.shape[0]
    bf16 = jnp.bfloat16
    sends = (groups + 2) * (2 * n_dev) + own_rows // SLAB + 1 + groups
    vmem = pl.BlockSpec(memory_space=pltpu.VMEM)
    smem = pl.BlockSpec(memory_space=pltpu.SMEM)
    anywhere = pl.BlockSpec(memory_space=pl.ANY)
    out = pl.pallas_call(
        functools.partial(kernel, n_dev, samples, slots, widths),
        out_shape=jax.ShapeDtypeStruct((own_rows, query_cols), bf16),
        in_specs=[anywhere] * 5 + [smem, anywhere],
        out_specs=vmem,
        scratch_shapes=[
            pltpu.VMEM((ctx_rows, features), bf16),
            pltpu.VMEM((features // HEAD_SIZE, HEAD_SIZE), jnp.float32),
            pltpu.VMEM((1, features), jnp.float32),
            pltpu.VMEM((samples, slots, slots), jnp.int32),
            pltpu.VMEM((2 * own_rows, features), bf16),
            pltpu.VMEM((ctx_rows, features), bf16),
            pltpu.VMEM((features, 2 * HEAD_SIZE), bf16),
        ]
        + [pltpu.VMEM((features, width * HEAD_SIZE), bf16) for width in widths]
        + [
            pltpu.VMEM((n_dev * ctx_rows, 2 * HEAD_SIZE), bf16),
            pltpu.VMEM((2, n_dev * ctx_rows + own_rows, 2 * HEAD_SIZE), bf16),
            pltpu.VMEM((max(widths), 2 * own_rows, HEAD_SIZE), bf16),
            pltpu.VMEM((2 * own_rows, 2 * slots), bf16),
            pltpu.VMEM((2 * own_rows, own_rows), jnp.float32),
            pltpu.VMEM((own_rows, query_cols // 2), bf16),
            pltpu.SemaphoreType.DMA((groups + 2, 2, n_dev)),
            pltpu.SemaphoreType.DMA((sends,)),
            pltpu.SemaphoreType.DMA((6 + groups,)),
            pltpu.SemaphoreType.DMA((own_rows // SLAB + 1,)),
            pltpu.SemaphoreType.DMA((groups,)),
        ],
        compiler_params=pltpu.CompilerParams(
            collective_id=0, has_side_effects=True, vmem_limit_bytes=62 * 1024 * 1024
        ),
        name="shared_context_attention",
    )(
        ctx_hidden, step_hidden.reshape(own_rows, features), norm_gain.reshape(features // HEAD_SIZE, HEAD_SIZE),
        w_query, w_keyval, step_lengths, step_mask,
    )
    return out.reshape(samples, slots, query_cols)


def solution(mesh):
    placed = (
        P("dev", None),
        P(("grp", "dev"), None, None),
        P(),
        P("dev", None),
        P("dev", None),
        P(("grp", "dev")),
        P(("grp", "dev"), None, None),
    )
    return jax.shard_map(
        functools.partial(local, n_dev=mesh.shape["dev"]),
        mesh=mesh, in_specs=placed, out_specs=P(("grp", "dev"), None, None), check_vma=False,
    )
```

time: 96.3 us -> 84.8 us (0.88); the launches traced: 96 us -> 83.1 us
  Pallas kernels: 88 us -> 81.1 us
  local copies, waits for them, and re-layouts: 7.91 us -> 1.99 us
    pallas_call x1, Pallas kernels: 88 us -> 81.1 us  [local(): pl.pallas_call(functools.partial(kernel, n_dev, samples, slots, widths),...]
    unnamed x13 -> x1, local copies, waits for them, and re-layouts: 7.19 us -> 1.99 us
where the time goes in v2:
time: 84.8 us; the launch traced here: 83.1 us
  Pallas kernels  81.1 us (96%)
  local copies, waits for them, and re-layouts  1.99 us (2%)
    pallas_call x1, Pallas kernels, local(): pl.pallas_call(functools.partial(kernel, n_dev, samples, slots, widths),...  81.1 us
    unnamed x1, local copies, waits for them, and re-layouts  1.99 us

profile of v2, /device:TPU:0, one launch (start us, length us, event | category | flops | bytes accessed | tf_op | source)
XLA Modules:
  0.0 83.1 jit_solution(9098028048493036216)
XLA Ops:
  0.0 81.1 %shared_context_attention.1 = bf16[192,1792]{1,0:T(8,128)(2,1)} custom-call(bf16[64,3584]{1,0:T(8,128)(2,1)} %ctx_hbm.1, bf16[192,3584]{1,0:T(8,128)(2,1)} %bitcast.4, f32[28,128]{1,0:T(8,128)} %bitcast.5, bf16[448,1792]{1,0:T(8,128)(2,1)} %wq_ref.1, bf16[448,512]{1,0:T(8,128)(2,1)} %wkv_ref.1, s32[3]{0:T(128)} %lens_ref.1, s32[3,64,64]{2,1,0:T(8,128)} %mask_hbm.1), custom_call_target="tpu_custom_call" | custom-call | tf_op jit(solution)/shard_map/shared_context_attention/pallas_call | solution.py:330
  81.1 2.0 %copy.9 = bf16[3,64,1792]{2,1,0:T(8,128)(2,1)} copy(bf16[3,64,1792]{2,1,0:T(8,128)(2,1)} %bitcast.3) | data formatting | bytes 1376256

commit v3 on v2

--- a/solution.py
+++ b/solution.py
@@ -58,8 +58,14 @@
     pair = (g + 2 - 4 * head, d)
     across = (g, 2 * a + 1 - b)
 
-    def along(t):
+    def along(j):
+        t = j + (a // (line // 2)) * (line - 2 * j)
         return 2 * lax.rem(a + t, line) + b
+
+    relayed = line > 2
+    at_end = (a == 0) | (a == line - 1)
+    before_end = (a == 1) | (a == line - 2)
+    end = (g, 2 * (a // (line // 2)) * (line - 1) + b)
 
     barrier = pltpu.get_barrier_semaphore()
     friends = [sibling, pair, across] + [(g, along(t)) for t in range(1, line)]
@@ -69,13 +75,16 @@
 
     pending = []
 
-    def send(src, dst, sem, target):
+    def send(src, dst, sem, target, cond=None):
         copy = pltpu.make_async_remote_copy(
             src_ref=src, dst_ref=dst, send_sem=send_sem.at[len(pending)], recv_sem=sem,
             device_id=target, device_id_type=MESH,
         )
-        copy.start()
-        pending.append(copy)
+        if cond is None:
+            copy.start()
+        else:
+            pl.when(cond)(copy.start)
+        pending.append((copy, cond))
 
     class Gather:
         def __init__(self, kind, buf, size):
@@ -95,25 +104,29 @@
             ref = self.at(src, half)
             pltpu.make_async_copy(ref, ref, self.sem(src, half)).wait()
 
-        def forward(self, src, target):
+        def forward(self, src, target, cond=None):
             ref = self.at(src, self.mine)
-            send(ref, ref, self.sem(src, self.mine), target)
-
-        def starts(self, source):
-            targets = [(g, along(t)) for t in range(1, line)]
-            targets.insert(1, across)
-            place, sem = self.at(d, self.mine), self.sem(d, self.mine)
-            return [functools.partial(send, source, place, sem, target) for target in targets]
+            send(ref, ref, self.sem(src, self.mine), target, cond)
+
+        def starts(self):
+            events = []
+            for j in range(1, line):
+                cond = jnp.logical_not(at_end) if relayed and j == line - 1 else None
+                events.append(functools.partial(self.forward, d, (g, along(j)), cond))
+            events.insert(1, functools.partial(self.forward, d, across))
+            return events
 
         def relay_along(self, t):
             src = along(t)
             self.wait(src, self.mine)
+            if relayed and t == line - 2:
+                self.forward(src, end, before_end)
             self.forward(src, across)
             if self.halves == 2:
                 self.forward(src, sibling)
 
         def relay_across(self, t):
-            src = 2 * lax.rem(a + t, line) + 1 - b
+            src = (d if t == 0 else along(t)) + 1 - 2 * b
             self.wait(src, self.mine)
             if self.halves == 2:
                 self.forward(src, sibling)
@@ -162,23 +175,20 @@
     for src, dst in small:
         local(src, dst)
     col = 0
-    starts = []
     for i in range(groups):
         width = widths[i] * HEAD_SIZE
         cols = pl.ds(pl.multiple_of(head * half_cols + col, HEAD_SIZE), width)
         local(wq_ref.at[:, cols], wq_bufs[i].at[own_shard])
-        starts.append(cols)
         col += width
     locals_[0].wait()
     locals_[1].wait()
-    pushes = []
-    for i in range(groups):
-        gather = gathers[1 + i]
-        first = pl.multiple_of(gather.mine * gather.piece, 16)
-        pushes.append(gather.starts(wq_ref.at[pl.ds(first, gather.piece), starts[i]]))
     pair_sends = [functools.partial(send_slab, i) for i in range(slabs)]
-    third = -(-slabs // 3)
-    run(gathers[0].starts(gathers[0].at(d, gathers[0].mine)) + pushes[0], pair_sends[:third])
+    run(gathers[0].starts(), pair_sends[:slabs // 3])
+    locals_[6].wait()
+    run(gathers[1].starts(), pair_sends[slabs // 3:])
+    for copy in locals_[7:]:
+        copy.wait()
+    pushes = [gather.starts() for gather in gathers[1:]]
 
     t_at = lax.broadcasted_iota(jnp.int32, (slots, slots), 0)
     u_at = lax.broadcasted_iota(jnp.int32, (slots, slots), 1)
@@ -263,14 +273,14 @@
     may_buf[...] = jnp.zeros_like(may_buf)
     expand(1)
     norm_rows(ctx_ref, ctx_buf, gain_ref, ctx_rows, 0)
-    run(gathers[0].along_line(), pushes[1], pair_sends[third:2 * third])
+    run(gathers[0].along_line(), pushes[1])
     locals_[2].wait()
     norm_rows(rows_buf, rows_buf, gain_ref, own_rows, own_rows)
-    run(gathers[0].across_line(), gathers[1].along_line(), pushes[2], pair_sends[2 * third:])
+    run(gathers[0].across_line(), gathers[1].along_line(), pushes[2])
     gathers[0].finish()
     own_ckv = jnp.dot(ctx_buf[...], wkv_buf[...], preferred_element_type=jnp.float32)
     ckv_buf[pl.ds(pl.multiple_of(d * ctx_rows, 16), ctx_rows), :] = own_ckv.astype(jnp.bfloat16)
-    run(ctx_gather.starts(ctx_gather.at(d, ctx_gather.mine)))
+    run(ctx_gather.starts())
     project_step(1)
     run(gathers[1].across_line(), ctx_gather.along_line(), gathers[2].along_line(), sum(pushes[3:], []))
     run(ctx_gather.across_line())
@@ -278,7 +288,6 @@
     for group in range(2):
         keyval_buf[group, pl.ds(0, all_ctx), :] = ckv_buf[...]
 
-    locals_[6].wait()
     gathers[1].finish()
     project_query(0, own_rows, own_rows)
     attend(0, 1)
@@ -297,7 +306,6 @@
     for i in range(1, groups):
         across_next = gathers[2 + i].across_line() if i + 1 < groups else []
         along_next = gathers[3 + i].along_line() if i + 2 < groups else []
-        locals_[6 + i].wait()
         gathers[1 + i].finish()
         project_query(i, 0, 2 * own_rows)
         run(across_next[:2], along_next[:2])
@@ -311,8 +319,11 @@
         here = out_ref.at[:, pl.ds(pl.multiple_of((1 - head) * half_cols + col, HEAD_SIZE), width)]
         pltpu.make_async_copy(here, here, out_recv.at[i]).wait()
         col += width
-    for copy in pending:
-        copy.wait_send()
+    for copy, cond in pending:
+        if cond is None:
+            copy.wait_send()
+        else:
+            pl.when(cond)(copy.wait_send)
 
 
 def local(ctx_hidden, step_hidden, norm_gain, w_query, w_keyval, step_lengths, step_mask, n_dev):

time: 84.8 us -> 75.2 us (0.89); the launches traced: 83.1 us -> 75 us
  Pallas kernels: 81.1 us -> 73 us
    pallas_call x1, Pallas kernels: 81.1 us -> 73 us  [local(): pl.pallas_call(functools.partial(kernel, n_dev, samples, slots, widths),...]
where the time goes in v3:
time: 75.2 us; the launch traced here: 75 us
  Pallas kernels  73 us (97%)
  local copies, waits for them, and re-layouts  1.99 us (3%)
    pallas_call x1, Pallas kernels, local(): pl.pallas_call(functools.partial(kernel, n_dev, samples, slots, widths),...  73 us
    unnamed x1, local copies, waits for them, and re-layouts  1.99 us

profile of v3, /device:TPU:0, one launch (start us, length us, event | category | flops | bytes accessed | tf_op | source)
XLA Modules:
  0.0 75.0 jit_solution(7343425290439480970)
XLA Ops:
  0.0 73.0 %shared_context_attention.1 = bf16[192,1792]{1,0:T(8,128)(2,1)} custom-call(bf16[64,3584]{1,0:T(8,128)(2,1)} %ctx_hbm.1, bf16[192,3584]{1,0:T(8,128)(2,1)} %bitcast.4, f32[28,128]{1,0:T(8,128)} %bitcast.5, bf16[448,1792]{1,0:T(8,128)(2,1)} %wq_ref.1, bf16[448,512]{1,0:T(8,128)(2,1)} %wkv_ref.1, s32[3]{0:T(128)} %lens_ref.1, s32[3,64,64]{2,1,0:T(8,128)} %mask_hbm.1), custom_call_target="tpu_custom_call" | custom-call | tf_op jit(solution)/shard_map/shared_context_attention/pallas_call | solution.py:341
  73.0 2.0 %copy.9 = bf16[3,64,1792]{2,1,0:T(8,128)(2,1)} copy(bf16[3,64,1792]{2,1,0:T(8,128)(2,1)} %bitcast.3) | data formatting | bytes 1376256

commit v4 on v3

--- a/solution.py
+++ b/solution.py
@@ -109,12 +109,35 @@
             send(ref, ref, self.sem(src, self.mine), target, cond)
 
         def starts(self):
+            events = self.to_line(d)
+            events.insert(1, functools.partial(self.forward, d, across))
+            return events
+
+        def to_line(self, src):
             events = []
             for j in range(1, line):
                 cond = jnp.logical_not(at_end) if relayed and j == line - 1 else None
-                events.append(functools.partial(self.forward, d, (g, along(j)), cond))
-            events.insert(1, functools.partial(self.forward, d, across))
+                events.append(functools.partial(self.forward, src, (g, along(j)), cond))
             return events
+
+        def spread_across(self):
+            src = d + 1 - 2 * b
+            self.wait(src, self.mine)
+            if self.halves == 2:
+                self.forward(src, sibling)
+            for event in self.to_line(src):
+                event()
+
+        def take_along(self, t, other):
+            src = along(t) + (1 - 2 * b if other else 0)
+            self.wait(src, self.mine)
+            if relayed and t == line - 2:
+                self.forward(src, end, before_end)
+            if self.halves == 2:
+                self.forward(src, sibling)
+
+        def take_line(self, other):
+            return [functools.partial(self.take_along, t, other) for t in range(1, line)]
 
         def relay_along(self, t):
             src = along(t)
@@ -182,6 +205,7 @@
         col += width
     locals_[0].wait()
     locals_[1].wait()
+    last = gathers[-1]
     pair_sends = [functools.partial(send_slab, i) for i in range(slabs)]
     run(gathers[0].starts(), pair_sends[:slabs // 3])
     locals_[6].wait()
@@ -283,6 +307,7 @@
     run(ctx_gather.starts())
     project_step(1)
     run(gathers[1].across_line(), ctx_gather.along_line(), gathers[2].along_line(), sum(pushes[3:], []))
+    last.spread_across()
     run(ctx_gather.across_line())
     ctx_gather.finish()
     for group in range(2):
@@ -304,8 +329,12 @@
     attend(0, 0)
 
     for i in range(1, groups):
-        across_next = gathers[2 + i].across_line() if i + 1 < groups else []
-        along_next = gathers[3 + i].along_line() if i + 2 < groups else []
+        across_next = gathers[2 + i].across_line() if i + 2 < groups else []
+        along_next = gathers[3 + i].along_line() if i + 3 < groups else []
+        if i + 2 == groups:
+            across_next = last.take_line(True)
+        if i + 3 == groups:
+            along_next = last.take_line(False)
         gathers[1 + i].finish()
         project_query(i, 0, 2 * own_rows)
         run(across_next[:2], along_next[:2])

time: 75.2 us -> 76.2 us (1.013)
  Pallas kernels: 73 us -> 74 us
    pallas_call x1, Pallas kernels: 73 us -> 74 us  [local(): pl.pallas_call(functools.partial(kernel, n_dev, samples, slots, widths),...]
where the time goes in v4:
time: 76.2 us; the launch traced here: 76 us
  Pallas kernels  74 us (97%)
  local copies, waits for them, and re-layouts  1.99 us (3%)
    pallas_call x1, Pallas kernels, local(): pl.pallas_call(functools.partial(kernel, n_dev, samples, slots, widths),...  74 us
    unnamed x1, local copies, waits for them, and re-layouts  1.99 us

profile of v4, /device:TPU:0, one launch (start us, length us, event | category | flops | bytes accessed | tf_op | source)
XLA Modules:
  0.0 76.0 jit_solution(790296855836543260)
XLA Ops:
  0.0 74.0 %shared_context_attention.1 = bf16[192,1792]{1,0:T(8,128)(2,1)} custom-call(bf16[64,3584]{1,0:T(8,128)(2,1)} %ctx_hbm.1, bf16[192,3584]{1,0:T(8,128)(2,1)} %bitcast.4, f32[28,128]{1,0:T(8,128)} %bitcast.5, bf16[448,1792]{1,0:T(8,128)(2,1)} %wq_ref.1, bf16[448,512]{1,0:T(8,128)(2,1)} %wkv_ref.1, s32[3]{0:T(128)} %lens_ref.1, s32[3,64,64]{2,1,0:T(8,128)} %mask_hbm.1), custom_call_target="tpu_custom_call" | custom-call | tf_op jit(solution)/shard_map/shared_context_attention/pallas_call | solution.py:370
  74.0 2.0 %copy.9 = bf16[3,64,1792]{2,1,0:T(8,128)(2,1)} copy(bf16[3,64,1792]{2,1,0:T(8,128)(2,1)} %bitcast.3) | data formatting | bytes 1376256

commit v5 on v3

--- a/solution.py
+++ b/solution.py
@@ -306,11 +306,12 @@
     for i in range(1, groups):
         across_next = gathers[2 + i].across_line() if i + 1 < groups else []
         along_next = gathers[3 + i].along_line() if i + 2 < groups else []
+        run(along_next)
         gathers[1 + i].finish()
         project_query(i, 0, 2 * own_rows)
-        run(across_next[:2], along_next[:2])
+        run(across_next[:2])
         attend(i, 0)
-        run(across_next[2:], along_next[2:])
+        run(across_next[2:])
         attend(i, 1)
 
     col = 0

time: 75.2 us -> 74.7 us (level)
  no operation moved by 1% of the time
where the time goes in v5:
time: 74.7 us; the launch traced here: 74.5 us
  Pallas kernels  72.5 us (97%)
  local copies, waits for them, and re-layouts  1.99 us (3%)
    pallas_call x1, Pallas kernels, local(): pl.pallas_call(functools.partial(kernel, n_dev, samples, slots, widths),...  72.5 us
    unnamed x1, local copies, waits for them, and re-layouts  1.99 us

profile of v5, /device:TPU:0, one launch (start us, length us, event | category | flops | bytes accessed | tf_op | source)
XLA Modules:
  0.0 74.5 jit_solution(16792406483458775762)
XLA Ops:
  0.0 72.5 %shared_context_attention.1 = bf16[192,1792]{1,0:T(8,128)(2,1)} custom-call(bf16[64,3584]{1,0:T(8,128)(2,1)} %ctx_hbm.1, bf16[192,3584]{1,0:T(8,128)(2,1)} %bitcast.4, f32[28,128]{1,0:T(8,128)} %bitcast.5, bf16[448,1792]{1,0:T(8,128)(2,1)} %wq_ref.1, bf16[448,512]{1,0:T(8,128)(2,1)} %wkv_ref.1, s32[3]{0:T(128)} %lens_ref.1, s32[3,64,64]{2,1,0:T(8,128)} %mask_hbm.1), custom_call_target="tpu_custom_call" | custom-call | tf_op jit(solution)/shard_map/shared_context_attention/pallas_call | solution.py:342
  72.5 2.0 %copy.9 = bf16[3,64,1792]{2,1,0:T(8,128)(2,1)} copy(bf16[3,64,1792]{2,1,0:T(8,128)(2,1)} %bitcast.3) | data formatting | bytes 1376256
